TPU v7x, 32 devices: a whole 2x2x4 slice. The times are simulated.
32 devices in a mesh: dp: 16 (over z, x, core), tensor: 2 (over y).
Axes of the slice: x: 2, y: 2, z: 4, core: 2. Of those that a mesh axis runs over, the one named last changes fastest.
Arguments:
- hidden: bfloat16 [32, 1024, 1024], P('dp'), may hold values from -6 to 6
- segment_ids: int32 [32, 1024], P('dp'), may hold values from 0 to 3, never falling along the last dimension, each value on 1 to 800 neighbouring positions
- norm_gain: float32 [1024], replicated, may hold values from 0.1 to 1.9
- proj_gate: bfloat16 [1024, 2048], P(None, 'tensor'), may hold values from -0.1875 to 0.1875
- proj_value: bfloat16 [1024, 2048], P(None, 'tensor'), may hold values from -0.1875 to 0.1875
- proj_state: bfloat16 [1024, 256], replicated, may hold values from -0.1875 to 0.1875
- proj_step: bfloat16 [1024, 32], P(None, 'tensor'), may hold values from -0.1875 to 0.1875
- conv_value: float32 [4, 2048], P(None, 'tensor'), may hold values from -3 to 3
- conv_value_bias: float32 [2048], P('tensor'), may hold values from -3 to 3
- conv_state: float32 [4, 256], replicated, may hold values from -3 to 3
- conv_state_bias: float32 [256], replicated, may hold values from -3 to 3
- step_bias: float32 [32], P('tensor'), may hold values from -6 to -2
- decay_log: float32 [32], P('tensor'), may hold values from 0 to 2.77
- skip_gain: float32 [32], P('tensor'), may hold values from 0.5 to 1.5
- gate_gain: float32 [2048], P('tensor'), may hold values from 0.1 to 1.9
- proj_out: bfloat16 [1024, 2048], P(None, 'tensor'), may hold values from -0.125 to 0.125
- out_grad: bfloat16 [32, 1024, 1024], P('dp'), may hold values from -6 to 6
Outputs:
- block_out: bfloat16 [32, 1024, 1024], P('dp')
- grad_hidden: float32 [32, 1024, 1024], P('dp')
- grad_norm_gain: float32 [1024], replicated
- grad_proj_gate: float32 [1024, 2048], P('dp', 'tensor')
- grad_proj_value: float32 [1024, 2048], P('dp', 'tensor')
- grad_proj_state: float32 [1024, 256], P('dp')
- grad_proj_step: float32 [1024, 32], P('dp', 'tensor')
- grad_conv_value: float32 [4, 2048], P(None, 'tensor')
- grad_conv_value_bias: float32 [2048], P('tensor')
- grad_conv_state: float32 [4, 256], replicated
- grad_conv_state_bias: float32 [256], replicated
- grad_step_bias: float32 [32], P('tensor')
- grad_decay_log: float32 [32], P('tensor')
- grad_skip_gain: float32 [32], P('tensor')
- grad_gate_gain: float32 [2048], P('tensor')
- grad_proj_out: float32 [1024, 2048], P('dp', 'tensor')
Inputs may be any that keep to these rules, and one draw needn't show every extreme that they name: `segment_ids`: tokens of a sequence with the same number form one document; numbers never fall along a sequence; each sequence holds 4 documents of 1 to 800 tokens, one of exactly 800.
All inputs are finite; a program needn't handle non-finite values.
Results may differ from a plain program's by a relative error of at most 0.019.
Values sent between devices are 32-bit elements; how exact they have to be, the bound alone decides.
A program may use at most 192 MiB of HBM per device.

v0:
```python
import functools
import jax
import jax.numpy as jnp
from jax import lax
from jax.sharding import PartitionSpec as P

HEAD_DIM = 64
STATE = 128
KERNEL = 4
epsilon = 1e-05
precise = lax.Precision.HIGHEST


def lag_masks(segment_row):
    length = segment_row.shape[0]
    result = [jnp.ones((length,), jnp.float32)]
    for delay in range(1, KERNEL):
        earlier = jnp.concatenate(
            [jnp.full((delay,), -1, jnp.int32), segment_row[: length - delay]]
        )
        result.append((earlier == segment_row).astype(jnp.float32))
    return result


def causal_conv(values, weight, conv_bias, doc_masks):
    length = values.shape[0]
    summed = conv_bias[None, :] + weight[KERNEL - 1][None, :] * values
    for delay in range(1, KERNEL):
        earlier = jnp.concatenate(
            [jnp.zeros((delay, values.shape[1]), jnp.float32), values[: length - delay]], axis=0
        )
        summed = summed + weight[KERNEL - 1 - delay][None, :] * earlier * doc_masks[delay][:, None]
    return jax.nn.silu(summed)


CHUNK = 128


def head_mix(values, states, step_raw, segment_row, step_bias, decay_log, skip_gain):
    length, inner = values.shape
    heads = step_raw.shape[1]
    chunks = length // CHUNK
    step_size = jax.nn.softplus(step_raw + step_bias[None, :])
    decay_rate = -jnp.exp(decay_log)
    places = jnp.arange(CHUNK)
    lower = places[:, None] >= places[None, :]
    drop = (step_size * decay_rate[None, :]).reshape(chunks, CHUNK, heads)
    running = jnp.einsum("ts,csh->cth", lower.astype(jnp.float32), drop, precision=precise)
    segments = segment_row.reshape(chunks, CHUNK)
    last = segments[:, -1]
    before = jnp.concatenate([jnp.full((1,), -1, jnp.int32), last[:-1]])
    allowed = lower[None] & (segments[:, :, None] == segments[:, None, :])
    state_in = states[:, :STATE].astype(jnp.bfloat16).reshape(chunks, CHUNK, STATE)
    state_out = states[:, STATE:].astype(jnp.bfloat16).reshape(chunks, CHUNK, STATE)
    affinity = jnp.einsum("ctn,csn->cts", state_out, state_in, preferred_element_type=jnp.float32)
    running_head = running.transpose(0, 2, 1)
    step_head = step_size.reshape(chunks, CHUNK, heads).transpose(0, 2, 1)
    decays = jnp.exp(
        jnp.where(
            allowed[:, None], running_head[:, :, :, None] - running_head[:, :, None, :], -1e30
        )
    )
    mixing = (decays * affinity[:, None] * step_head[:, :, None, :]).astype(jnp.bfloat16)
    low_head = values.astype(jnp.bfloat16).reshape(chunks, CHUNK, heads, HEAD_DIM)
    near = jnp.einsum("chts,cshp->cthp", mixing, low_head, preferred_element_type=jnp.float32)
    near = near.reshape(chunks, CHUNK, inner)
    spread = (jnp.arange(inner)[None, :] // HEAD_DIM == jnp.arange(heads)[:, None]).astype(
        jnp.float32
    )
    total = running[:, -1, :]
    at_end = (segments == last[:, None]).astype(jnp.float32)
    from_start = (segments == before[:, None]).astype(jnp.float32)
    keep_scale = (
        jnp.exp(total[:, None, :] - running)
        * step_size.reshape(chunks, CHUNK, heads)
        * at_end[:, :, None]
    )
    read_scale = jnp.exp(running) * from_start[:, :, None]
    carry = jnp.exp(total) * (last == before).astype(jnp.float32)[:, None]
    keep_wide = jnp.einsum("cth,hi->cti", keep_scale, spread, precision=lax.Precision.HIGH)
    read_wide = jnp.einsum("cth,hi->cti", read_scale, spread, precision=lax.Precision.HIGH)
    carry_wide = jnp.einsum("ch,hi->ci", carry, spread, precision=precise)
    kept = (values.reshape(chunks, CHUNK, inner) * keep_wide).astype(jnp.bfloat16)
    gained = jnp.einsum("csn,csi->cni", state_in, kept, preferred_element_type=jnp.float32)
    held = jnp.zeros((STATE, inner), jnp.float32)
    entry = []
    for c in range(chunks):
        entry.append(held.astype(jnp.bfloat16))
        held = held * carry_wide[c][None, :] + gained[c]
    entry = jnp.stack(entry)
    far = jnp.einsum("ctn,cni->cti", state_out, entry, preferred_element_type=jnp.float32)
    mixed = (near + far * read_wide).reshape(length, inner)
    return mixed + jnp.repeat(skip_gain, HEAD_DIM)[None, :] * values


def mixer(
    segment_row,
    value_row,
    state_row,
    step_row,
    conv_value,
    conv_value_bias,
    conv_state,
    conv_state_bias,
    step_bias,
    decay_log,
    skip_gain,
):
    doc_masks = lag_masks(segment_row)
    value_conv = causal_conv(value_row, conv_value, conv_value_bias, doc_masks)
    state_conv = causal_conv(state_row, conv_state, conv_state_bias, doc_masks)
    return head_mix(value_conv, state_conv, step_row, segment_row, step_bias, decay_log, skip_gain)


def right_product(left, weight):
    return lax.dot_general(
        left, weight, (((1,), (1,)), ((), ())), preferred_element_type=jnp.float32
    )


def token_product(left, right):
    return lax.dot_general(
        left, right, (((0,), (0,)), ((), ())), preferred_element_type=jnp.float32
    )


def tensor_others(part):
    count = lax.axis_size("tensor")
    if count == 2:
        return lax.ppermute(part, "tensor", [(0, 1), (1, 0)])
    return lax.psum(part, "tensor")


def tensor_join(part, others):
    return part + others if lax.axis_size("tensor") == 2 else others


def after(value, *earlier):
    return lax.optimization_barrier((value, *earlier))[0]


def local(
    hidden,
    segment_ids,
    norm_gain,
    proj_gate,
    proj_value,
    proj_state,
    proj_step,
    conv_value,
    conv_value_bias,
    conv_state,
    conv_state_bias,
    step_bias,
    decay_log,
    skip_gain,
    gate_gain,
    proj_out,
    out_grad,
):
    seq_count, length, width = hidden.shape
    local_inner = proj_gate.shape[1]
    local_heads = proj_step.shape[1]
    state_width = proj_state.shape[1]
    tensor_count = lax.axis_size("tensor")
    inner_total = local_inner * tensor_count
    every = range(seq_count)
    wides = [hidden[s].astype(jnp.float32) for s in every]
    row_scales = [lax.rsqrt(jnp.mean(w * w, axis=-1, keepdims=True) + epsilon) for w in wides]
    normeds = [(w * r * norm_gain[None, :]).astype(jnp.bfloat16) for w, r in zip(wides, row_scales)]
    params = (
        conv_value,
        conv_value_bias,
        conv_state,
        conv_state_bias,
        step_bias,
        decay_log,
        skip_gain,
    )
    gate_raws, mixed_outs, mixer_backs, gateds, squares = ([], [], [], [], [])
    for s in every:
        gate_raw = jnp.dot(normeds[s], proj_gate, preferred_element_type=jnp.float32)
        value_raw = jnp.dot(normeds[s], proj_value, preferred_element_type=jnp.float32)
        state_raw = jnp.dot(normeds[s], proj_state, preferred_element_type=jnp.float32)
        step_raw = jnp.dot(normeds[s], proj_step, preferred_element_type=jnp.float32)
        mixed_out, back = jax.vjp(
            jax.checkpoint(functools.partial(mixer, segment_ids[s])),
            value_raw,
            state_raw,
            step_raw,
            *params
        )
        gated = mixed_out * jax.nn.silu(gate_raw)
        gate_raws.append(gate_raw)
        mixed_outs.append(mixed_out)
        mixer_backs.append(back)
        gateds.append(gated)
        squares.append(jnp.sum(gated * gated, axis=-1))
    d_output_ins = [
        jnp.dot(out_grad[s], proj_out, preferred_element_type=jnp.float32) for s in every
    ]
    inners = [jnp.sum(d_output_ins[s] * gate_gain[None, :] * gateds[s], axis=-1) for s in every]
    both = lax.psum(jnp.stack(squares + inners), "tensor")
    branches, received, output_ins, d_gates, d_mixeds = ([], [], [], [], [])
    grad_gate_gain = jnp.zeros((local_inner,), jnp.float32)
    for s in every:
        gated, gate_raw = (gateds[s], gate_raws[s])
        gated_scale = lax.rsqrt(both[s] / inner_total + epsilon)[:, None]
        gate_inner = both[seq_count + s][:, None]
        output_in = (gated * gated_scale * gate_gain[None, :]).astype(jnp.bfloat16)
        branches.append(right_product(output_in, proj_out))
        received.append(tensor_others(branches[s]))
        d_output_in = d_output_ins[s]
        grad_gate_gain = grad_gate_gain + jnp.sum(d_output_in * gated * gated_scale, axis=0)
        weighted = d_output_in * gate_gain[None, :]
        d_gated = gated_scale * weighted - gated_scale**3 * gated * gate_inner / inner_total
        sigma = jax.nn.sigmoid(gate_raw)
        d_mixeds.append(d_gated * gate_raw * sigma)
        d_gates.append(
            (d_gated * mixed_outs[s] * sigma * (1.0 + gate_raw * (1.0 - sigma))).astype(
                jnp.bfloat16
            )
        )
        output_ins.append(output_in)
    normed_all = jnp.concatenate(normeds, axis=0)
    early_part = jnp.concatenate(
        [
            token_product(normed_all, jnp.concatenate(d_gates, axis=0)),
            token_product(
                out_grad.reshape(seq_count * length, width), jnp.concatenate(output_ins, axis=0)
            ),
        ],
        axis=1,
    )
    early = lax.psum_scatter(early_part, "dp", scatter_dimension=0, tiled=True)
    late_weight = jnp.concatenate([proj_value, proj_state, proj_step], axis=1)
    param_grads, lates, parts, others, grad_hiddens = (None, [], [], [], [])
    waits = (early_part, *branches)
    grad_norm_gain = jnp.zeros((width,), jnp.float32)
    for s in every:
        d_value, d_state, d_step, *grads = mixer_backs[s](after(d_mixeds[s], *waits))
        param_grads = grads if s == 0 else [a + b for a, b in zip(param_grads, grads)]
        late = jnp.concatenate([d_value, d_state, d_step], axis=1).astype(jnp.bfloat16)
        lates.append(late)
        part = right_product(d_gates[s], proj_gate) + right_product(late, late_weight)
        grad_norm_gain = grad_norm_gain + jnp.sum(part * wides[s] * row_scales[s], axis=0)
        parts.append(part)
        if s < seq_count - 1:
            parts[s] = after(part, received[s])
            others.append(tensor_others(parts[s]))
            waits = (part, received[s])
    edge_state = local_inner + state_width
    g_cv, g_cvb, g_cs, g_csb, g_sb, g_dl, g_sg = param_grads
    own = [g_cv, g_cvb, g_sb, g_dl, g_sg, grad_gate_gain]
    shared = [g_cs, g_csb, grad_norm_gain]
    own_flat = jnp.concatenate([g.reshape(-1) for g in own])
    place = lax.axis_index("tensor")
    mine = (jnp.arange(tensor_count) == place)[:, None]
    slots = jnp.where(mine, own_flat[None, :], 0.0).reshape(-1)
    packed = lax.psum(
        after(
            jnp.concatenate([slots] + [g.reshape(-1) for g in shared]), early, received[-1], *others
        ),
        ("dp", "tensor"),
    )
    own_sum = lax.dynamic_slice(packed, (place * own_flat.shape[0],), (own_flat.shape[0],))
    shared_sum = packed[slots.shape[0] :]
    later = lax.psum_scatter(
        token_product(normed_all, after(jnp.concatenate(lates, axis=0), packed)),
        "dp",
        scatter_dimension=0,
        tiled=True,
    )
    block_outs = []
    for s in every:
        if s == seq_count - 1:
            parts[s] = after(parts[s], packed)
            others.append(tensor_others(parts[s]))
        d_scaled = tensor_join(parts[s], others[s]) * norm_gain[None, :]
        row_scale, wide = (row_scales[s], wides[s])
        norm_inner = jnp.sum(d_scaled * wide, axis=-1, keepdims=True)
        grad_hiddens.append(
            out_grad[s].astype(jnp.float32)
            + row_scale * d_scaled
            - row_scale**3 * wide * norm_inner / width
        )
        branch = tensor_join(branches[s], received[s])
        block_outs.append((wide + branch).astype(jnp.bfloat16))
    grad_proj_state = lax.psum(later[:, local_inner:edge_state], "tensor")

    def split(flat, like):
        result, edge = ([], 0)
        for g in like:
            result.append(flat[edge : edge + g.size].reshape(g.shape))
            edge += g.size
        return result

    r_cv, r_cvb, r_sb, r_dl, r_sg, r_gg = split(own_sum, own)
    r_cs, r_csb, r_ng = split(shared_sum, shared)
    return (
        jnp.stack(block_outs),
        jnp.stack(grad_hiddens),
        r_ng,
        early[:, :local_inner],
        later[:, :local_inner],
        grad_proj_state,
        later[:, edge_state:],
        r_cv,
        r_cvb,
        r_cs,
        r_csb,
        r_sb,
        r_dl,
        r_sg,
        r_gg,
        early[:, local_inner:],
    )


def solution(mesh):
    in_specs = (
        P("dp", None, None),
        P("dp", None),
        P(),
        P(None, "tensor"),
        P(None, "tensor"),
        P(),
        P(None, "tensor"),
        P(None, "tensor"),
        P("tensor"),
        P(),
        P(),
        P("tensor"),
        P("tensor"),
        P("tensor"),
        P("tensor"),
        P(None, "tensor"),
        P("dp", None, None),
    )
    out_specs = (
        P("dp", None, None),
        P("dp", None, None),
        P(),
        P("dp", "tensor"),
        P("dp", "tensor"),
        P("dp", None),
        P("dp", "tensor"),
        P(None, "tensor"),
        P("tensor"),
        P(),
        P(),
        P("tensor"),
        P("tensor"),
        P("tensor"),
        P("tensor"),
        P("dp", "tensor"),
    )
    return jax.shard_map(local, mesh=mesh, in_specs=in_specs, out_specs=out_specs, check_vma=False)
```

profile of v0, /device:TPU:0, one launch (start us, length us, event | category | flops | bytes accessed | tf_op | source)
XLA Modules:
  0.0 794.7 jit_solution(9242613608619532424)
XLA Ops:
  50.2 22.6 %fusion.435 = (bf16[1024,1024]{1,0:T(8,128)(2,1)}, f32[1024,1024]{1,0:T(8,128)}, bf16[1024,1024]{1,0:T(8,128)(2,1)}, f32[1024,1024]{1,0:T(8,128)S(1)}) fusion(f32[1024]{0:T(1024)S(1)} %get-tuple-element.468, f32[1021,1024]{1,0:T(8,128)} %bitcast.722, f32[1024]{0:T(1024)S(1)} %bitcast.950, f32[1024]{0:T(1024)S(1)} %get-tuple-element.467, ...), kind=kLoop, calls=%fused_computation.717 | loop fusion | flops 33554432 | bytes 46133248 | tf_op jit(solution)/shard_map/jvp()/convert_element_type | solution.py:64
  79.6 6.4 reshape.1877
  87.0 7.6 fusion.19
  109.9 6.5 reshape.1876
  116.5 7.6 fusion.18
  144.4 14.7 %multiply_reduce_fusion.15 = (f32[1024]{0:T(1024)S(1)}, f32[1024]{0:T(1024)S(1)}, f32[1024,1024]{1,0:T(8,128)}, f32[1024]{0:T(1024)S(1)}, f32[1024]{0:T(1024)S(1...) fusion(f32[1024]{0:T(1024)S(1)} %copy-done.208, f32[1024,1024]{1,0:T(8,128)} %fusion.465, ...), kind=kOutput, calls=%fused_computation.169 | convolution fusion | flops 2172645376 | bytes 46161920 | tf_op jit(solution)/shard_map/dot_general | solution.py:200
  159.1 9.7 %psum.21 = f32[4,1024]{1,0:T(4,128)S(1)} all-reduce(f32[4,1024]{1,0:T(4,128)S(1)} %pad_maximum_fusion.9), channel_id=1, replica_groups=mesh['dp'=16,'tensor'=2] {'tensor'}, use_global_device_ids=true, to_apply=%region_6.7 | all-reduce | flops 4096 | bytes 32768 | tf_op jit(solution)/shard_map/psum | solution.py:203
  168.9 19.2 %multiply_multiply_fusion.1 = (f32[1024,1024]{1,0:T(8,128)}, bf16[1024,1024]{1,0:T(8,128)(2,1)S(1)}, f32[1024]{0:T(1024)}, bf16[1024,1024]{1,0:T(8,128)(2,1)S(1)...) fusion(f32[1024,1024]{1,0:T(8,128)} %fusion.465, ...), kind=kLoop, calls=%fused_computation.152 | loop fusion | flops 54523904 | bytes 58761216 | tf_op jit(solution)/shard_map/mul | solution.py:218
  208.3 9.2 %copy.351 = f32[1024,2048]{1,0:T(8,128)} copy(f32[1024,2048]{0,1:T(8,128)} %pad_maximum_fusion) | data formatting | bytes 16777216
  248.1 13.2 %multiply_reduce_fusion.3 = (f32[1024]{0:T(1024)}, f32[1024,1024]{1,0:T(8,128)S(1)}, f32[1024,1024]{1,0:T(8,128)}) fusion(f32[1024,1024]{1,0:T(8,128)} %get-tuple-element.53, f32[1024]{0:T(1024)} %copy-done.130, f32[1021,1024]{1,0:T(8,128)} %bitcast.725, f32[1024]{0:T(1024)} %bitcast.927, f32[1024]{0:T(1024)} %copy-done.125, f32[1022,1024]{1,0:T(8,128)} %bitcast.726, ...), kind=kLoop, calls=%fused_computation.115 | loop fusion | flops 17824768 | bytes 29372416 | tf_op jit(solution)/shard_map/transpose(jvp(jvp()))/checkpoint/reduce_sum | solution.py:93
  287.4 7.3 copy.345
  294.8 7.7 reshape.1878
  305.1 11.4 %multiply_reduce_fusion.11 = (f32[1024]{0:T(1024)}, f32[1024,1024]{1,0:T(8,128)S(1)}, f32[1024,1024]{1,0:T(8,128)}) fusion(f32[1021,1024]{1,0:T(8,128)} %bitcast.728, f32[1024]{0:T(1024)} %copy-done.130, f32[1024,1024]{1,0:T(8,128)} %get-tuple-element.223, f32[1024,1024]{1,0:T(8,128)} %reshape.1878, f32[8,128,1024]{2,1,0:T(8,128)} %get-tuple-element.312, ...), kind=kLoop, calls=%fused_computation.123 | loop fusion | flops 15727616 | bytes 29360128 | tf_op jit(solution)/shard_map/transpose(jvp(jvp()))/checkpoint/reduce_sum | solution.py:32
  319.4 6.4 reshape.1879
  325.8 12.3 %fusion.15 = (f32[8,16,128]{2,1,0:T(8,128)}, f32[8,16,128]{2,1,0:T(8,128)}, f32[8,16,128]{2,1,0:T(8,128)S(1)}, bf16[8,128,128]{2,1,0:T(8,128)(2,1)S(1)}) fusion(f32[8,16,128]{2,1,0:T(8,128)} %copy.296, f32[8,128,128]{2,1,0:T(8,128)} %fusion.476, f32[8,16,128]{2,1,0:T(8,128)S(1)} %fusion.291, pred[8,128,128]{2,1,0:T(8,128)(4,1)} %compare_and_fusion.1, ...), kind=kOutput, calls=%fused_computation.39 | convolution fusion | flops 297615360 | bytes 5439488 | tf_op jit(solution)/shard_map/transpose(jvp(jvp()))/checkpoint/chts,cshp->cthp/dot_general | solution.py:65
  385.5 8.5 %fusion.135 = f32[1024,1024]{1,0:T(8,128)} fusion(f32[1024,1024]{1,0:T(8,128)} %fusion.475, bf16[1024,16]{1,0:T(8,128)(2,1)S(1)} %get-tuple-element.227, bf16[1024,256]{1,0:T(8,128)(2,1)S(1)} %get-tuple-element.318, bf16[1024,1024]{1,0:T(8,128)(2,1)S(1)} %get-tuple-element.304, bf16[1024,16]{1,0:T(8,128)(2,1)S(1)} %copy-done.96, ...), kind=kOutput, calls=%fused_computation.223 | convolution fusion | flops 2734882816 | bytes 13697024 | tf_op jit(solution)/shard_map/dot_general | solution.py:116
  414.1 7.1 copy.348
  421.2 7.6 reshape.1880
  438.3 13.2 %multiply_reduce_fusion.2 = (f32[1024]{0:T(1024)}, f32[1024,1024]{1,0:T(8,128)S(1)}, f32[1024,1024]{1,0:T(8,128)}) fusion(f32[1024,1024]{1,0:T(8,128)} %get-tuple-element.69, f32[1024]{0:T(1024)} %copy-done.128, f32[1021,1024]{1,0:T(8,128)} %bitcast.716, f32[1024]{0:T(1024)} %bitcast.925, f32[1024]{0:T(1024)} %copy-done.120, f32[1022,1024]{1,0:T(8,128)} %bitcast.717, ...), kind=kLoop, calls=%fused_computation.114 | loop fusion | flops 17824768 | bytes 29372416 | tf_op jit(solution)/shard_map/transpose(jvp(jvp()))/checkpoint/reduce_sum | solution.py:93
  455.2 6.4 reshape.1881
  461.6 11.3 %fusion.17 = (f32[8,16,128]{2,1,0:T(8,128)}, f32[8,16,128]{2,1,0:T(8,128)}, f32[8,16,128]{2,1,0:T(8,128)S(1)}, bf16[8,128,128]{2,1,0:T(8,128)(2,1)}) fusion(f32[8,16,128]{2,1,0:T(8,128)S(1)} %copy-done.141, f32[8,128,128]{2,1,0:T(8,128)S(1)} %fusion.480, f32[8,16,128]{2,1,0:T(8,128)S(1)} %fusion.288, pred[8,128,128]{2,1,0:T(8,128)(4,1)S(1)} %copy-done.105, ...), kind=kOutput, calls=%fused_computation.41 | convolution fusion | flops 297615360 | bytes 5439488 | tf_op jit(solution)/shard_map/transpose(jvp(jvp()))/checkpoint/chts,cshp->cthp/dot_general | solution.py:65
  500.0 9.2 %multiply_reduce_fusion.7 = (f32[1024]{0:T(1024)S(1)}, f32[1024,1024]{1,0:T(8,128)S(1)}, f32[1024,1024]{1,0:T(8,128)S(1)}) fusion(f32[1021,1024]{1,0:T(8,128)} %bitcast.719, f32[1024]{0:T(1024)S(1)} %copy-done.129, f32[1024,1024]{1,0:T(8,128)} %get-tuple-element.220, f32[1024,1024]{1,0:T(8,128)} %reshape.1880, f32[8,128,1024]{2,1,0:T(8,128)} %get-tuple-element.308, ...), kind=kLoop, calls=%fused_computation.119 | loop fusion | flops 15727616 | bytes 29360128 | tf_op jit(solution)/shard_map/transpose(jvp(jvp()))/checkpoint/reduce_sum | solution.py:32
  526.3 9.6 %fusion.44 = (f32[1024]{0:T(1024)S(1)}, f32[1024]{0:T(1024)S(1)}, f32[1024,1024]{1,0:T(8,128)}) fusion(f32[1024]{0:T(1024)S(1)} %copy-done.152, bf16[2,1024,1024]{2,1,0:T(8,128)(2,1)} %param.18, f32[1024]{0:T(1024)S(1)} %copy-done.154, f32[1024,1024]{1,0:T(8,128)} %fusion.135, f32[1024,1024]{1,0:T(8,128)} %fusion.479, bf16[1024,16]{1,0:T(8,128)(2,1)} %copy.309, ...), kind=kOutput, calls=%fused_computation.75 | convolution fusion | flops 2743269376 | bytes 22102016 | tf_op jit(solution)/shard_map/dot_general | solution.py:116
  536.0 26.3 %maximum_maximum_fusion = bf16[2048,1296]{1,0:T(8,128)(2,1)} fusion(bf16[1024,16]{1,0:T(8,128)(2,1)} %get-tuple-element.225, bf16[1024,256]{1,0:T(8,128)(2,1)S(1)} %get-tuple-element.319, bf16[1024,1024]{1,0:T(8,128)(2,1)} %get-tuple-element.305, bf16[1024,16]{1,0:T(8,128)(2,1)S(1)} %get-tuple-element.227, bf16[1024,256]{1,0:T(8,128)(2,1)S(1)} %copy-done.63, ...), kind=kLoop, calls=%fused_computation.44 | loop fusion | flops 31850496 | bytes 10616832 | tf_op jit(solution)/shard_map/concatenate | solution.py:269
  563.7 25.9 %collective-permute-done.2 = f32[1024,1024]{1,0:T(8,128)} collective-permute-done((f32[1024,1024]{1,0:T(8,128)}, f32[1024,1024]{1,0:T(8,128)}, u32[]{:S(2)}, u32[]{:S(2)}) %collective-permute-start.2) | collective-permute-done | bytes 4194336 | tf_op jit(solution)/shard_map/ppermute | solution.py:130
  589.6 40.5 %psum.22 = f32[14688]{0:T(1024)S(1)} all-reduce(f32[14688]{0:T(1024)S(1)} %concatenate.230), channel_id=1, replica_groups=mesh['dp'=16,'tensor'=2] {'dp','tensor'}, use_global_device_ids=true, to_apply=%region_65.67 | all-reduce | flops 14688 | bytes 117504 | tf_op jit(solution)/shard_map/psum | solution.py:260
  630.2 11.5 %fusion.112 = f32[1024,1296]{1,0:T(8,128)} fusion(bf16[2048,1296]{1,0:T(8,128)(2,1)} %maximum_maximum_fusion, bf16[1024,1024]{1,0:T(8,128)(2,1)} %copy-done.43, bf16[1024,1024]{1,0:T(8,128)(2,1)S(1)} %copy-done.42), kind=kOutput, calls=%fused_computation.204 | convolution fusion | flops 5444206592 | bytes 14811136 | tf_op jit(solution)/shard_map/dot_general | solution.py:122
  649.3 84.6 %collective-permute-done.3 = f32[1024,1024]{1,0:T(8,128)} collective-permute-done((f32[1024,1024]{1,0:T(8,128)}, f32[1024,1024]{1,0:T(8,128)}, u32[]{:S(2)}, u32[]{:S(2)}) %collective-permute-start.3) | collective-permute-done | bytes 4194336 | tf_op jit(solution)/shard_map/ppermute | solution.py:130
  734.0 11.7 %fusion.36 = (f32[1024]{0:T(1024)S(1)}, f32[1024]{0:T(1024)S(1)}, bf16[1,1024,1024]{2,1,0:T(8,128)(2,1)}) fusion(f32[1024]{0:T(1024)S(1)} %copy-done.148, f32[1024,1024]{1,0:T(8,128)} %fusion.135, f32[1024,1024]{1,0:T(8,128)} %collective-permute-done.2, bf16[2,1024,1024]{2,1,0:T(8,128)(2,1)} %param.18, f32[1024,1024]{1,0:T(8,128)} %get-tuple-element.82, ...), kind=kLoop, calls=%fused_computation.67 | loop fusion | flops 13629440 | bytes 31469568 | tf_op jit(solution)/shard_map/reduce_sum | solution.py:281
  745.8 11.8 %fusion.35 = (f32[1,1024,1024]{2,1,0:T(8,128)S(1)}, f32[1,1024,1024]{2,1,0:T(8,128)}, bf16[1,1024,1024]{2,1,0:T(8,128)(2,1)}) fusion(f32[1024]{0:T(1024)S(1)} %get-tuple-element.178, f32[1024]{0:T(1024)S(1)} %copy-done.176, f32[1024]{0:T(1024)S(1)} %copy-done.154, bf16[2,1024,1024]{2,1,0:T(8,128)(2,1)} %param.34, f32[1024]{0:T(1024)S(1)} %copy-done.148, ...), kind=kLoop, calls=%fused_computation.66 | loop fusion | flops 24117248 | bytes 44068864 | tf_op jit(solution)/shard_map/stack | solution.py:302
  757.5 6.8 pad_maximum_fusion.1
  772.1 14.4 %all-reduce.96.cloned.1.call-done = f32[64,256]{1,0:T(8,128)} async-done(((f32[64,256]{1,0:T(8,128)}), f32[64,256]{1,0:T(8,128)}) %all-reduce.96.cloned.1.call-update) | async-done | bytes 65552 | tf_op jit(solution)/shard_map/psum | solution.py:289
  (758 shorter events, 309.5 us)
Async XLA Ops:
  7.2 122.4 %copy-start = (bf16[1024,1024]{1,0:T(8,128)(2,1)S(1)}, bf16[1024,1024]{1,0:T(8,128)(2,1)}, u32[]{:S(2)}) copy-start(bf16[1024,1024]{1,0:T(8,128)(2,1)} %param.33) | copy-start | bytes 6291460
  7.2 555.1 %reduce-scatter.7.cloned.1.call-start = ((), (), s32[]{:S(2)}) async-start(), calls=%async_computation.4 | async-start | bytes 8912896
  8.1 77.9 %copy-start.72 = (s32[1,1024]{1,0:T(1,128)}, s32[1,1024]{1,0:T(1,128)S(1)}, u32[]{:S(2)}) copy-start(s32[1,1024]{1,0:T(1,128)S(1)} %get-tuple-element.415) | copy-start | bytes 12292
  16.0 14.7 %copy-start.40 = (bf16[1024,1024]{1,0:T(8,128)(2,1)}, bf16[1024,1024]{1,0:T(8,128)(2,1)S(1)}, u32[]{:S(2)}) copy-start(bf16[1024,1024]{1,0:T(8,128)(2,1)S(1)} %get-tuple-element.300) | copy-start | bytes 6291460
  16.0 19.0 %copy-start.43 = (bf16[1024,1024]{1,0:T(8,128)(2,1)}, bf16[1024,1024]{1,0:T(8,128)(2,1)S(1)}, u32[]{:S(2)}) copy-start(bf16[1024,1024]{1,0:T(8,128)(2,1)S(1)} %get-tuple-element.301) | copy-start | bytes 6291460
  26.3 13.8 %copy-start.75 = (f32[1024,16]{0,1:T(8,128)}, f32[1024,16]{0,1:T(8,128)S(1)}, u32[]{:S(2)}) copy-start(f32[1024,16]{0,1:T(8,128)S(1)} %fusion.467) | copy-start | bytes 196612
  28.9 12.8 %copy-start.5 = (f32[1024,256]{1,0:T(8,128)}, f32[1024,256]{1,0:T(8,128)S(1)}, u32[]{:S(2)}) copy-start(f32[1024,256]{1,0:T(8,128)S(1)} %fusion.468) | copy-start | bytes 3145732
  29.9 195.1 %copy-start.94 = (pred[128,128]{1,0:T(8,128)(4,1)}, pred[128,128]{1,0:T(8,128)(4,1)S(1)}, u32[]{:S(2)}) copy-start(pred[128,128]{1,0:T(8,128)(4,1)S(1)} %iota_compare_fusion.7) | copy-start | bytes 49156
  50.2 22.6 %copy-start.179 = (f32[8,16]{1,0:T(8,128)S(1)}, f32[8,16]{1,0:T(8,128)}, u32[]{:S(2)}) copy-start(f32[8,16]{1,0:T(8,128)} %copy-done.178) | copy-start | bytes 1540
  192.6 201.4 %collective-permute-start = (f32[1024,1024]{1,0:T(8,128)}, f32[1024,1024]{1,0:T(8,128)}, u32[]{:S(2)}, u32[]{:S(2)}) collective-permute-start(f32[1024,1024]{1,0:T(8,128)} %fusion.473), channel_id=1, source_target_pairs={{0,1},{1,0},{2,3},{3,2},{4,5},{5,4},{6,7},{7,6},{8,9},{9,8},{10,11... | collective-permute-start | bytes 12582920 | tf_op jit(solution)/shard_map/ppermute | solution.py:130
  217.6 546.8 %reduce-scatter.5.cloned.1.call-start = ((), (), s32[]{:S(2)}) async-start(), calls=%async_computation.2 | async-start | bytes 6127616 | tf_op jit(solution)/shard_map/reduce_scatter | solution.py:268
  223.7 340.0 %collective-permute-start.1 = (f32[1024,1024]{1,0:T(8,128)}, f32[1024,1024]{1,0:T(8,128)}, u32[]{:S(2)}, u32[]{:S(2)}) collective-permute-start(f32[1024,1024]{1,0:T(8,128)} %fusion.474), channel_id=1, source_target_pairs={{0,1},{1,0},{2,3},{3,2},{4,5},{5,4},{6,7},{7,6},{8,9},{9,8},{10,11... | collective-permute-start | bytes 12582920 | tf_op jit(solution)/shard_map/ppermute | solution.py:130
  305.1 11.4 %copy-start.162 = (f32[1,1024]{1,0:T(1,128)S(1)}, f32[1,1024]{1,0:T(1,128)}, u32[]{:S(2)}) copy-start(f32[1,1024]{1,0:T(1,128)} %get-tuple-element.390) | copy-start | bytes 12292
  325.8 12.4 %copy-start.53 = (bf16[1024,128]{1,0:T(8,128)(2,1)S(1)}, bf16[1024,128]{1,0:T(8,128)(2,1)}, u32[]{:S(2)}) copy-start(bf16[1024,128]{1,0:T(8,128)(2,1)} %copy-done.51) | copy-start | bytes 786436
  325.8 12.6 %copy-start.14 = (f32[8,128,1024]{2,1,0:T(8,128)S(1)}, f32[8,128,1024]{2,1,0:T(8,128)}, u32[]{:S(2)}) copy-start(f32[8,128,1024]{2,1,0:T(8,128)} %fusion.477) | copy-start | bytes 12582916
  325.8 12.6 %copy-start.107 = (f32[1,1024]{1,0:T(1,128)S(1)}, f32[1,1024]{1,0:T(1,128)}, u32[]{:S(2)}) copy-start(f32[1,1024]{1,0:T(1,128)} %get-tuple-element.361) | copy-start | bytes 12292
  325.8 12.6 %copy-start.109 = (f32[1,1024]{1,0:T(1,128)S(1)}, f32[1,1024]{1,0:T(1,128)}, u32[]{:S(2)}) copy-start(f32[1,1024]{1,0:T(1,128)} %get-tuple-element.362) | copy-start | bytes 12292
  325.8 12.6 %copy-start.111 = (f32[1,1024]{1,0:T(1,128)S(1)}, f32[1,1024]{1,0:T(1,128)}, u32[]{:S(2)}) copy-start(f32[1,1024]{1,0:T(1,128)} %get-tuple-element.364) | copy-start | bytes 12292
  325.8 12.6 %copy-start.113 = (f32[1,1024]{1,0:T(1,128)S(1)}, f32[1,1024]{1,0:T(1,128)}, u32[]{:S(2)}) copy-start(f32[1,1024]{1,0:T(1,128)} %get-tuple-element.366) | copy-start | bytes 12292
  363.7 21.7 %copy-start.62 = (bf16[1024,256]{1,0:T(8,128)(2,1)}, bf16[1024,256]{1,0:T(8,128)(2,1)S(1)}, u32[]{:S(2)}) copy-start(bf16[1024,256]{1,0:T(8,128)(2,1)S(1)} %get-tuple-element.318) | copy-start | bytes 1572868
  461.6 11.6 %copy-start.116 = (f32[1,1024]{1,0:T(1,128)S(1)}, f32[1,1024]{1,0:T(1,128)}, u32[]{:S(2)}) copy-start(f32[1,1024]{1,0:T(1,128)} %get-tuple-element.357) | copy-start | bytes 12292
  499.2 90.4 %collective-permute-start.2 = (f32[1024,1024]{1,0:T(8,128)}, f32[1024,1024]{1,0:T(8,128)}, u32[]{:S(2)}, u32[]{:S(2)}) collective-permute-start(f32[1024,1024]{1,0:T(8,128)} %fusion.135), channel_id=1, source_target_pairs={{0,1},{1,0},{2,3},{3,2},{4,5},{5,4},{6,7},{7,6},{8,9},{9,8},{10,11... | collective-permute-start | bytes 12582920 | tf_op jit(solution)/shard_map/ppermute | solution.py:130
  536.0 94.1 %copy-start.42 = (bf16[1024,1024]{1,0:T(8,128)(2,1)S(1)}, bf16[1024,1024]{1,0:T(8,128)(2,1)}, u32[]{:S(2)}) copy-start(bf16[1024,1024]{1,0:T(8,128)(2,1)} %copy-done.40) | copy-start | bytes 6291460
  641.7 92.3 %copy-start.148 = (f32[1024]{0:T(1024)S(1)}, f32[1024]{0:T(1024)}, u32[]{:S(2)}) copy-start(f32[1024]{0:T(1024)} %param.20) | copy-start | bytes 12292
  641.7 144.8 %all-reduce.96.cloned.1.call-start = ((), (), s32[]{:S(2)}) async-start(), calls=%async_computation.3 | async-start | bytes 131072 | tf_op jit(solution)/shard_map/psum | solution.py:289
  642.0 92.0 %collective-permute-start.3 = (f32[1024,1024]{1,0:T(8,128)}, f32[1024,1024]{1,0:T(8,128)}, u32[]{:S(2)}, u32[]{:S(2)}) collective-permute-start(f32[1024,1024]{1,0:T(8,128)} %get-tuple-element.82), channel_id=1, source_target_pairs={{0,1},{1,0},{2,3},{3,2},{4,5},{5,4},{6,7},{7,6},{8,9},{9,8},{10,11... | collective-permute-start | bytes 12582920 | tf_op jit(solution)/shard_map/ppermute | solution.py:130
  649.3 96.4 %copy-start.9 = (bf16[2,1024,1024]{2,1,0:T(8,128)(2,1)S(1)}, bf16[2,1024,1024]{2,1,0:T(8,128)(2,1)}, u32[]{:S(2)}) copy-start(bf16[2,1024,1024]{2,1,0:T(8,128)(2,1)} %param.18) | copy-start | bytes 12582916
  649.3 96.4 %copy-start.25 = (f32[1024,1024]{1,0:T(8,128)S(1)}, f32[1024,1024]{1,0:T(8,128)}, u32[]{:S(2)}) copy-start(f32[1024,1024]{1,0:T(8,128)} %fusion.135) | copy-start | bytes 12582916
  649.3 96.4 %copy-start.26 = (f32[1024,1024]{1,0:T(8,128)S(1)}, f32[1024,1024]{1,0:T(8,128)}, u32[]{:S(2)}) copy-start(f32[1024,1024]{1,0:T(8,128)} %get-tuple-element.82) | copy-start | bytes 12582916
  649.3 96.4 %copy-start.175 = (f32[1024]{0:T(1024)S(1)}, f32[1024]{0:T(1024)}, u32[]{:S(2)}) copy-start(f32[1024]{0:T(1024)} %get-tuple-element.420) | copy-start | bytes 12292
  649.3 96.4 %copy-start.176 = (f32[1024]{0:T(1024)S(1)}, f32[1024]{0:T(1024)}, u32[]{:S(2)}) copy-start(f32[1024]{0:T(1024)} %get-tuple-element.466) | copy-start | bytes 12292
  765.9 22.1 %copy-start.1 = (bf16[1024,1024]{1,0:T(8,128)(2,1)S(1)}, bf16[1024,1024]{1,0:T(8,128)(2,1)}, u32[]{:S(2)}) copy-start(bf16[1024,1024]{1,0:T(8,128)(2,1)} %param.33) | copy-start | bytes 6291460
  (213 other events, 838.3 us)
Sparse Core Ops, SparseCore 0:
  217.7 105.6 reduce-scatter.6
  641.8 81.9 reduce-scatter.4
  766.0 20.4 all-reduce.95
where the time goes:
time: 806 us; the launch traced here: 795 us
  other arithmetic  237 us (29%)
  matrix products  220 us (27%)
  local copies, waits for them, and re-layouts  142 us (18%)
  waiting for transfers between devices  125 us (16%)
  blocking collectives  50.2 us (6%)
  between operations  16.9 us (2%)
    ppermute x4, waiting for transfers between devices, tensor_others(): return lax.ppermute(part, 'tensor', [(0, 1), (1, 0)])  111 us
    dot_general x6, matrix products, head_mix(): jnp.einsum('chts,cshp->cthp', mixing, low_head, preferred_element_type=jn...  50.7 us
    psum x1, blocking collectives, local(): lax.psum(after(jnp.concatenate([slots] + [g.reshape(-1) for g in shared])...  40.5 us
    unnamed x495, local copies, waits for them, and re-layouts  39.8 us
    dot_general x6, matrix products, right_product(): lax.dot_general(left, weight, (((1,), (1,)), ((), ())), preferred_element...  37.4 us
    reduce_sum x8, other arithmetic, causal_conv(): weight[KERNEL - 1 - delay][None, :] * earlier * doc_masks[delay][:, None]  30.8 us
    convert_element_type x4, local copies, waits for them, and re-layouts, head_mix(): values.astype(jnp.bfloat16).reshape(chunks, CHUNK, heads, HEAD_DIM)  29.8 us
    reduce_sum x4, other arithmetic, head_mix(): return mixed + jnp.repeat(skip_gain, HEAD_DIM)[None, :] * values  27.3 us
  transfers between devices with their start and end apart: 7, of which 3 were waited for; matrix products, arithmetic and copies ran while one was open for 50% of the time, Pallas kernels for 0%

commit v1 on v0

--- a/solution.py
+++ b/solution.py
@@ -9,6 +9,15 @@
 KERNEL = 4
 epsilon = 1e-05
 precise = lax.Precision.HIGHEST
+
+
+def _convert_loops(buf, mesh_name):
+    p_next = jax.lax.all_gather(buf, mesh_name)
+    tall = jnp.sum(p_next, 0)
+    return tall
+
+
+work_the_works = functools.partial(_convert_loops, mesh_name=("dp", "tensor"))
 
 
 def lag_masks(segment_row):
@@ -257,11 +266,10 @@
     place = lax.axis_index("tensor")
     mine = (jnp.arange(tensor_count) == place)[:, None]
     slots = jnp.where(mine, own_flat[None, :], 0.0).reshape(-1)
-    packed = lax.psum(
+    packed = work_the_works(
         after(
             jnp.concatenate([slots] + [g.reshape(-1) for g in shared]), early, received[-1], *others
-        ),
-        ("dp", "tensor"),
+        )
     )
     own_sum = lax.dynamic_slice(packed, (place * own_flat.shape[0],), (own_flat.shape[0],))
     shared_sum = packed[slots.shape[0] :]

time: 806 us -> 903 us (1.12)
  waiting for transfers between devices: 125 us -> 243 us
  blocking collectives: 50.2 us -> 9.67 us
  local copies, waits for them, and re-layouts: 142 us -> 159 us
    unnamed x4 -> x6, waiting for transfers between devices: 0.05 us -> 119 us
    psum x1 -> x0, blocking collectives: 40.5 us -> none  [local(): lax.psum(after(jnp.concatenate([slots] + [g.reshape(-1) for g in shared])...]
    concatenate x1, other arithmetic: 26.3 us -> 14 us  [local(): jnp.concatenate(lates, axis=0)]
    reshape x2, local copies, waits for them, and re-layouts: 10.9 us -> 21.6 us  [head_mix(): near = near.reshape(chunks, CHUNK, inner)]
    mul x12, other arithmetic: 11.4 us -> 20.8 us  [causal_conv(): weight[KERNEL - 1 - delay][None, :] * earlier * doc_masks[delay][:, None]]
    unnamed x495 -> x499, local copies, waits for them, and re-layouts: 39.8 us -> 44.9 us
  transfers between devices with their start and end apart: 7 -> 8, of which waited for: 3 -> 4; matrix products, arithmetic and copies ran while one was open for 50% -> 44% of each run, Pallas kernels for 0% -> 0%
where the time goes in v1:
time: 903 us; the launch traced here: 892 us
  waiting for transfers between devices  243 us (27%)
  other arithmetic  238 us (26%)
  matrix products  222 us (25%)
  local copies, waits for them, and re-layouts  159 us (18%)
  between operations  17 us (2%)
  blocking collectives  9.67 us (1%)
    unnamed x6, waiting for transfers between devices  119 us
    ppermute x4, waiting for transfers between devices, tensor_others(): return lax.ppermute(part, 'tensor', [(0, 1), (1, 0)])  110 us
    dot_general x6, matrix products, head_mix(): jnp.einsum('chts,cshp->cthp', mixing, low_head, preferred_element_type=jn...  50.7 us
    unnamed x499, local copies, waits for them, and re-layouts  44.9 us
    dot_general x6, matrix products, right_product(): lax.dot_general(left, weight, (((1,), (1,)), ((), ())), preferred_element...  36.8 us
    convert_element_type x4, local copies, waits for them, and re-layouts, head_mix(): values.astype(jnp.bfloat16).reshape(chunks, CHUNK, heads, HEAD_DIM)  29.8 us
    reduce_sum x8, other arithmetic, causal_conv(): weight[KERNEL - 1 - delay][None, :] * earlier * doc_masks[delay][:, None]  29.6 us
    reduce_sum x4, other arithmetic, head_mix(): return mixed + jnp.repeat(skip_gain, HEAD_DIM)[None, :] * values  27.6 us
  transfers between devices with their start and end apart: 8, of which 4 were waited for; matrix products, arithmetic and copies ran while one was open for 44% of the time, Pallas kernels for 0%

profile of v1, /device:TPU:0, one launch (start us, length us, event | category | flops | bytes accessed | tf_op | source)
XLA Modules:
  0.0 891.8 jit_solution(17091183046651739956)
XLA Ops:
  50.3 21.8 %fusion.435 = (bf16[1024,1024]{1,0:T(8,128)(2,1)}, f32[1024,1024]{1,0:T(8,128)}, bf16[1024,1024]{1,0:T(8,128)(2,1)}, f32[1024,1024]{1,0:T(8,128)S(1)}) fusion(f32[1024]{0:T(1024)S(1)} %get-tuple-element.468, f32[1021,1024]{1,0:T(8,128)} %bitcast.722, f32[1024]{0:T(1024)S(1)} %bitcast.950, f32[1024]{0:T(1024)S(1)} %get-tuple-element.467, ...), kind=kLoop, calls=%fused_computation.717 | loop fusion | flops 33554432 | bytes 46133248 | tf_op jit(solution)/shard_map/jvp()/convert_element_type | solution.py:73
  86.3 7.6 fusion.19
  93.9 16.3 %copy.290 = f32[8,128,1024]{2,1,0:T(8,128)} copy(f32[8,128,1024]{1,2,0:T(8,128)} %bitcast.774) | data formatting | bytes 8388608 | tf_op jit(solution)/shard_map/jvp()/reshape | solution.py:75
  126.4 7.6 fusion.18
  154.3 14.7 %multiply_reduce_fusion.15 = (f32[1024]{0:T(1024)S(1)}, f32[1024]{0:T(1024)S(1)}, f32[1024,1024]{1,0:T(8,128)}, f32[1024]{0:T(1024)S(1)}, f32[1024]{0:T(1024)S(1...) fusion(f32[1024]{0:T(1024)S(1)} %copy-done.203, f32[1024,1024]{1,0:T(8,128)} %fusion.465, ...), kind=kOutput, calls=%fused_computation.169 | convolution fusion | flops 2172645376 | bytes 46161920 | tf_op jit(solution)/shard_map/dot_general | solution.py:209
  169.0 9.7 %psum.14 = f32[4,1024]{1,0:T(4,128)S(1)} all-reduce(f32[4,1024]{1,0:T(4,128)S(1)} %pad_maximum_fusion.9), channel_id=1, replica_groups=mesh['dp'=16,'tensor'=2] {'tensor'}, use_global_device_ids=true, to_apply=%region_6.7 | all-reduce | flops 4096 | bytes 32768 | tf_op jit(solution)/shard_map/psum | solution.py:212
  178.8 19.2 %multiply_multiply_fusion.1 = (f32[1024,1024]{1,0:T(8,128)}, bf16[1024,1024]{1,0:T(8,128)(2,1)S(1)}, f32[1024]{0:T(1024)}, bf16[1024,1024]{1,0:T(8,128)(2,1)S(1)...) fusion(f32[1024,1024]{1,0:T(8,128)} %fusion.465, ...), kind=kLoop, calls=%fused_computation.152 | loop fusion | flops 54523904 | bytes 58761216 | tf_op jit(solution)/shard_map/mul | solution.py:227
  218.2 9.1 %copy.351 = f32[1024,2048]{1,0:T(8,128)} copy(f32[1024,2048]{0,1:T(8,128)} %pad_maximum_fusion) | data formatting | bytes 16777216
  257.8 13.3 %multiply_reduce_fusion.3 = (f32[1024]{0:T(1024)}, f32[1024,1024]{1,0:T(8,128)S(1)}, f32[1024,1024]{1,0:T(8,128)}) fusion(f32[1024,1024]{1,0:T(8,128)} %get-tuple-element.53, f32[1024]{0:T(1024)} %copy-done.123, f32[1021,1024]{1,0:T(8,128)} %bitcast.725, f32[1024]{0:T(1024)} %bitcast.927, f32[1024]{0:T(1024)} %copy-done.120, f32[1022,1024]{1,0:T(8,128)} %bitcast.726, ...), kind=kLoop, calls=%fused_computation.115 | loop fusion | flops 17824768 | bytes 29372416 | tf_op jit(solution)/shard_map/transpose(jvp(jvp()))/checkpoint/reduce_sum | solution.py:102
  297.2 7.3 copy.345
  304.6 7.7 reshape.1881
  314.9 11.4 %multiply_reduce_fusion.11 = (f32[1024]{0:T(1024)}, f32[1024,1024]{1,0:T(8,128)S(1)}, f32[1024,1024]{1,0:T(8,128)}) fusion(f32[1021,1024]{1,0:T(8,128)} %bitcast.728, f32[1024]{0:T(1024)} %copy-done.123, f32[1024,1024]{1,0:T(8,128)} %get-tuple-element.223, f32[1024,1024]{1,0:T(8,128)} %reshape.1881, f32[8,128,1024]{2,1,0:T(8,128)} %get-tuple-element.312, ...), kind=kLoop, calls=%fused_computation.123 | loop fusion | flops 15727616 | bytes 29360128 | tf_op jit(solution)/shard_map/transpose(jvp(jvp()))/checkpoint/reduce_sum | solution.py:41
  335.6 12.3 %fusion.15 = (f32[8,16,128]{2,1,0:T(8,128)}, f32[8,16,128]{2,1,0:T(8,128)}, f32[8,16,128]{2,1,0:T(8,128)S(1)}, bf16[8,128,128]{2,1,0:T(8,128)(2,1)S(1)}) fusion(f32[8,16,128]{2,1,0:T(8,128)} %copy.296, f32[8,128,128]{2,1,0:T(8,128)} %fusion.476, f32[8,16,128]{2,1,0:T(8,128)S(1)} %fusion.291, pred[8,128,128]{2,1,0:T(8,128)(4,1)} %compare_and_fusion.1, ...), kind=kOutput, calls=%fused_computation.39 | convolution fusion | flops 297615360 | bytes 5439488 | tf_op jit(solution)/shard_map/transpose(jvp(jvp()))/checkpoint/chts,cshp->cthp/dot_general | solution.py:74
  394.7 8.4 fusion.135
  420.6 13.4 %multiply_reduce_fusion.2 = (f32[1024]{0:T(1024)}, f32[1024,1024]{1,0:T(8,128)S(1)}, f32[1024,1024]{1,0:T(8,128)}) fusion(f32[1024,1024]{1,0:T(8,128)} %get-tuple-element.69, f32[1024]{0:T(1024)S(1)} %get-tuple-element.431, f32[1021,1024]{1,0:T(8,128)} %bitcast.716, f32[1024]{0:T(1024)S(1)} %bitcast.925, f32[1024]{0:T(1024)S(1)} %get-tuple-element.432, ...), kind=kLoop, calls=%fused_computation.114 | loop fusion | flops 17824768 | bytes 29372416 | tf_op jit(solution)/shard_map/transpose(jvp(jvp()))/checkpoint/reduce_sum | solution.py:102
  456.5 7.1 copy.348
  463.6 7.6 reshape.1883
  472.0 6.7 reshape.1884
  478.7 11.2 %fusion.17 = (f32[8,16,128]{2,1,0:T(8,128)}, f32[8,16,128]{2,1,0:T(8,128)}, f32[8,16,128]{2,1,0:T(8,128)S(1)}, bf16[8,128,128]{2,1,0:T(8,128)(2,1)S(1)}) fusion(f32[8,16,128]{2,1,0:T(8,128)S(1)} %copy.315, f32[8,128,128]{2,1,0:T(8,128)S(1)} %copy-done.92, f32[8,16,128]{2,1,0:T(8,128)S(1)} %fusion.288, pred[8,128,128]{2,1,0:T(8,128)(4,1)S(1)} %compare_and_fusion, ...), kind=kOutput, calls=%fused_computation.41 | convolution fusion | flops 297615360 | bytes 5439488 | tf_op jit(solution)/shard_map/transpose(jvp(jvp()))/checkpoint/chts,cshp->cthp/dot_general | solution.py:74
  516.0 7.0 multiply_reduce_fusion.7
  523.0 6.7 slice_multiply_fusion.2
  540.8 8.5 fusion.421
  550.8 9.2 %fusion.44 = (f32[1024]{0:T(1024)S(1)}, f32[1024]{0:T(1024)S(1)}, f32[1024,1024]{1,0:T(8,128)}) fusion(f32[1024]{0:T(1024)S(1)} %copy-done.143, bf16[2,1024,1024]{2,1,0:T(8,128)(2,1)} %param.18, f32[1024]{0:T(1024)S(1)} %copy-done.145, f32[1024,1024]{1,0:T(8,128)} %fusion.135, f32[1024,1024]{1,0:T(8,128)} %fusion.479, bf16[1024,16]{1,0:T(8,128)(2,1)} %copy.309, ...), kind=kOutput, calls=%fused_computation.75 | convolution fusion | flops 2743269376 | bytes 22102016 | tf_op jit(solution)/shard_map/dot_general | solution.py:125
  561.7 23.7 %collective-permute-done.2 = f32[1024,1024]{1,0:T(8,128)} collective-permute-done((f32[1024,1024]{1,0:T(8,128)}, f32[1024,1024]{1,0:T(8,128)}, u32[]{:S(2)}, u32[]{:S(2)}) %collective-permute-start.2) | collective-permute-done | bytes 4194336 | tf_op jit(solution)/shard_map/ppermute | solution.py:139
  588.5 14.0 %maximum_maximum_fusion = bf16[2048,1296]{1,0:T(8,128)(2,1)} fusion(bf16[1024,16]{1,0:T(8,128)(2,1)} %copy-done.86, bf16[1024,256]{1,0:T(8,128)(2,1)} %get-tuple-element.319, bf16[1024,1024]{1,0:T(8,128)(2,1)} %copy-done.52, bf16[1024,16]{1,0:T(8,128)(2,1)S(1)} %copy-done.85, bf16[1024,256]{1,0:T(8,128)(2,1)} %copy-done.73, bf16[1024,1024]{1,0:T(8,128)(2,1)S(1)} %copy-done.51), kind=kLoop, calls=%fused_computation.44 | loop fusion | flops 31850496 | bytes 10616832 | tf_op jit(solution)/shard_map/concatenate | solution.py:277
  602.5 119.3 %all-reduce.100.cloned.1.call-done = f32[470016]{0:T(1024)} async-done(((f32[470016]{0:T(1024)}), f32[470016]{0:T(1024)}) %all-reduce.100.cloned.1.call-update) | async-done | bytes 1880080
  727.3 11.6 %fusion.112 = f32[1024,1296]{1,0:T(8,128)} fusion(bf16[2048,1296]{1,0:T(8,128)(2,1)} %maximum_maximum_fusion, bf16[1024,1024]{1,0:T(8,128)(2,1)} %copy-done.48, bf16[1024,1024]{1,0:T(8,128)(2,1)S(1)} %copy-done.47), kind=kOutput, calls=%fused_computation.204 | convolution fusion | flops 5444206592 | bytes 14811136 | tf_op jit(solution)/shard_map/dot_general | solution.py:131
  745.4 86.0 %collective-permute-done.3 = f32[1024,1024]{1,0:T(8,128)} collective-permute-done((f32[1024,1024]{1,0:T(8,128)}, f32[1024,1024]{1,0:T(8,128)}, u32[]{:S(2)}, u32[]{:S(2)}) %collective-permute-start.3) | collective-permute-done | bytes 4194336 | tf_op jit(solution)/shard_map/ppermute | solution.py:139
  831.4 12.0 %fusion.36 = (f32[1024]{0:T(1024)S(1)}, f32[1024]{0:T(1024)S(1)}, bf16[1,1024,1024]{2,1,0:T(8,128)(2,1)}) fusion(f32[1024]{0:T(1024)S(1)} %copy-done.138, f32[1024,1024]{1,0:T(8,128)} %fusion.135, f32[1024,1024]{1,0:T(8,128)} %collective-permute-done.2, bf16[2,1024,1024]{2,1,0:T(8,128)(2,1)} %param.18, f32[1024,1024]{1,0:T(8,128)} %get-tuple-element.82, ...), kind=kLoop, calls=%fused_computation.67 | loop fusion | flops 13629440 | bytes 31469568 | tf_op jit(solution)/shard_map/reduce_sum | solution.py:289
  843.5 11.8 %fusion.35 = (f32[1,1024,1024]{2,1,0:T(8,128)S(1)}, f32[1,1024,1024]{2,1,0:T(8,128)}, bf16[1,1024,1024]{2,1,0:T(8,128)(2,1)}) fusion(f32[1024]{0:T(1024)S(1)} %get-tuple-element.178, f32[1024]{0:T(1024)S(1)} %copy-done.172, f32[1024]{0:T(1024)S(1)} %copy-done.145, bf16[2,1024,1024]{2,1,0:T(8,128)(2,1)} %param.34, f32[1024]{0:T(1024)S(1)} %copy-done.138, ...), kind=kLoop, calls=%fused_computation.66 | loop fusion | flops 24117248 | bytes 44068864 | tf_op jit(solution)/shard_map/stack | solution.py:310
  855.2 6.8 pad_maximum_fusion.1
  869.8 13.6 %all-reduce.98.cloned.1.call-done = f32[64,256]{1,0:T(8,128)} async-done(((f32[64,256]{1,0:T(8,128)}), f32[64,256]{1,0:T(8,128)}) %all-reduce.98.cloned.1.call-update) | async-done | bytes 65552 | tf_op jit(solution)/shard_map/psum | solution.py:297
  (766 shorter events, 332.1 us)
Async XLA Ops:
  7.2 132.3 %copy-start = (bf16[1024,1024]{1,0:T(8,128)(2,1)S(1)}, bf16[1024,1024]{1,0:T(8,128)(2,1)}, u32[]{:S(2)}) copy-start(bf16[1024,1024]{1,0:T(8,128)(2,1)} %param.33) | copy-start | bytes 6291460
  7.2 553.0 %reduce-scatter.7.cloned.1.call-start = ((), (), s32[]{:S(2)}) async-start(), calls=%async_computation.5 | async-start | bytes 8912896
  8.1 77.2 %copy-start.80 = (s32[1,1024]{1,0:T(1,128)}, s32[1,1024]{1,0:T(1,128)S(1)}, u32[]{:S(2)}) copy-start(s32[1,1024]{1,0:T(1,128)S(1)} %get-tuple-element.415) | copy-start | bytes 12292
  16.0 19.1 %copy-start.48 = (bf16[1024,1024]{1,0:T(8,128)(2,1)}, bf16[1024,1024]{1,0:T(8,128)(2,1)S(1)}, u32[]{:S(2)}) copy-start(bf16[1024,1024]{1,0:T(8,128)(2,1)S(1)} %get-tuple-element.301) | copy-start | bytes 6291460
  30.0 204.7 %copy-start.98 = (pred[128,128]{1,0:T(8,128)(4,1)}, pred[128,128]{1,0:T(8,128)(4,1)S(1)}, u32[]{:S(2)}) copy-start(pred[128,128]{1,0:T(8,128)(4,1)S(1)} %iota_compare_fusion.7) | copy-start | bytes 49156
  50.3 21.8 %copy-start.175 = (f32[8,16]{1,0:T(8,128)S(1)}, f32[8,16]{1,0:T(8,128)}, u32[]{:S(2)}) copy-start(f32[8,16]{1,0:T(8,128)} %copy-done.174) | copy-start | bytes 1540
  93.9 16.7 %copy-start.79 = (bf16[1024,256]{1,0:T(8,128)(2,1)S(1)}, bf16[1024,256]{1,0:T(8,128)(2,1)}, u32[]{:S(2)}) copy-start(bf16[1024,256]{1,0:T(8,128)(2,1)} %get-tuple-element.416) | copy-start | bytes 1572868
  93.9 16.8 %copy-start.225 = (f32[8]{0:T(128)S(1)}, f32[8]{0:T(128)}, u32[]{:S(2)}) copy-start(f32[8]{0:T(128)} %get-tuple-element.472) | copy-start | bytes 100
  93.9 17.0 %copy-start.201 = (s32[8,1]{0,1:T(1,128)S(1)}, s32[8,1]{0,1:T(1,128)}, u32[]{:S(2)}) copy-start(s32[8,1]{0,1:T(1,128)} %copy-done.200) | copy-start | bytes 100
  93.9 17.0 %copy-start.219 = (s32[8]{0:T(128)S(1)}, s32[8]{0:T(128)}, u32[]{:S(2)}) copy-start(s32[8]{0:T(128)} %get-tuple-element.471) | copy-start | bytes 100
  202.4 200.8 %collective-permute-start = (f32[1024,1024]{1,0:T(8,128)}, f32[1024,1024]{1,0:T(8,128)}, u32[]{:S(2)}, u32[]{:S(2)}) collective-permute-start(f32[1024,1024]{1,0:T(8,128)} %fusion.473), channel_id=1, source_target_pairs={{0,1},{1,0},{2,3},{3,2},{4,5},{5,4},{6,7},{7,6},{8,9},{9,8},{10,11... | collective-permute-start | bytes 12582920 | tf_op jit(solution)/shard_map/ppermute | solution.py:139
  227.4 494.4 %all-reduce.100.cloned.1.call-start = ((), (), s32[]{:S(2)}) async-start(), calls=%async_computation.4 | async-start | bytes 3760128
  233.5 328.2 %collective-permute-start.1 = (f32[1024,1024]{1,0:T(8,128)}, f32[1024,1024]{1,0:T(8,128)}, u32[]{:S(2)}, u32[]{:S(2)}) collective-permute-start(f32[1024,1024]{1,0:T(8,128)} %fusion.474), channel_id=1, source_target_pairs={{0,1},{1,0},{2,3},{3,2},{4,5},{5,4},{6,7},{7,6},{8,9},{9,8},{10,11... | collective-permute-start | bytes 12582920 | tf_op jit(solution)/shard_map/ppermute | solution.py:139
  373.5 21.1 %copy-start.73 = (bf16[1024,256]{1,0:T(8,128)(2,1)}, bf16[1024,256]{1,0:T(8,128)(2,1)S(1)}, u32[]{:S(2)}) copy-start(bf16[1024,256]{1,0:T(8,128)(2,1)S(1)} %get-tuple-element.318) | copy-start | bytes 1572868
  374.7 20.0 %copy-start.84 = (bf16[1024,16]{1,0:T(8,128)(2,1)}, bf16[1024,16]{1,0:T(8,128)(2,1)S(1)}, u32[]{:S(2)}) copy-start(bf16[1024,16]{1,0:T(8,128)(2,1)S(1)} %get-tuple-element.227) | copy-start | bytes 98308
  406.1 91.8 %copy-start.53 = (bf16[1024,128]{1,0:T(8,128)(2,1)}, bf16[1024,128]{1,0:T(8,128)(2,1)S(1)}, u32[]{:S(2)}) copy-start(bf16[1024,128]{1,0:T(8,128)(2,1)S(1)} %get-tuple-element.329) | copy-start | bytes 786436
  419.2 74.8 %copy-start.125 = (f32[8,16]{1,0:T(8,128)}, f32[8,16]{1,0:T(8,128)S(1)}, u32[]{:S(2)}) copy-start(f32[8,16]{1,0:T(8,128)S(1)} %slice_reduce_fusion) | copy-start | bytes 1540
  420.5 69.7 %copy-start.82 = (f32[8,128,16]{1,2,0:T(8,128)}, f32[8,128,16]{1,2,0:T(8,128)S(1)}, u32[]{:S(2)}) copy-start(f32[8,128,16]{1,2,0:T(8,128)S(1)} %copy.313) | copy-start | bytes 196612
  495.0 90.4 %collective-permute-start.2 = (f32[1024,1024]{1,0:T(8,128)}, f32[1024,1024]{1,0:T(8,128)}, u32[]{:S(2)}, u32[]{:S(2)}) collective-permute-start(f32[1024,1024]{1,0:T(8,128)} %fusion.135), channel_id=1, source_target_pairs={{0,1},{1,0},{2,3},{3,2},{4,5},{5,4},{6,7},{7,6},{8,9},{9,8},{10,11... | collective-permute-start | bytes 12582920 | tf_op jit(solution)/shard_map/ppermute | solution.py:139
  560.0 28.4 %copy-start.51 = (bf16[1024,1024]{1,0:T(8,128)(2,1)S(1)}, bf16[1024,1024]{1,0:T(8,128)(2,1)}, u32[]{:S(2)}) copy-start(bf16[1024,1024]{1,0:T(8,128)(2,1)} %copy-done.50) | copy-start | bytes 6291460
  560.0 28.4 %copy-start.85 = (bf16[1024,16]{1,0:T(8,128)(2,1)S(1)}, bf16[1024,16]{1,0:T(8,128)(2,1)}, u32[]{:S(2)}) copy-start(bf16[1024,16]{1,0:T(8,128)(2,1)} %copy-done.84) | copy-start | bytes 98308
  588.4 273.7 %reduce-scatter.5.cloned.1.call-start = ((), (), s32[]{:S(2)}) async-start(), calls=%async_computation.2 | async-start | bytes 6127616 | tf_op jit(solution)/shard_map/reduce_scatter | solution.py:276
  602.5 124.9 %copy-start.47 = (bf16[1024,1024]{1,0:T(8,128)(2,1)S(1)}, bf16[1024,1024]{1,0:T(8,128)(2,1)}, u32[]{:S(2)}) copy-start(bf16[1024,1024]{1,0:T(8,128)(2,1)} %copy-done.45) | copy-start | bytes 6291460
  738.9 92.6 %copy-start.138 = (f32[1024]{0:T(1024)S(1)}, f32[1024]{0:T(1024)}, u32[]{:S(2)}) copy-start(f32[1024]{0:T(1024)} %param.20) | copy-start | bytes 12292
  738.9 144.5 %all-reduce.98.cloned.1.call-start = ((), (), s32[]{:S(2)}) async-start(), calls=%async_computation.3 | async-start | bytes 131072 | tf_op jit(solution)/shard_map/psum | solution.py:297
  739.0 92.5 %collective-permute-start.3 = (f32[1024,1024]{1,0:T(8,128)}, f32[1024,1024]{1,0:T(8,128)}, u32[]{:S(2)}, u32[]{:S(2)}) collective-permute-start(f32[1024,1024]{1,0:T(8,128)} %get-tuple-element.82), channel_id=1, source_target_pairs={{0,1},{1,0},{2,3},{3,2},{4,5},{5,4},{6,7},{7,6},{8,9},{9,8},{10,11... | collective-permute-start | bytes 12582920 | tf_op jit(solution)/shard_map/ppermute | solution.py:139
  745.4 98.0 %copy-start.9 = (bf16[2,1024,1024]{2,1,0:T(8,128)(2,1)S(1)}, bf16[2,1024,1024]{2,1,0:T(8,128)(2,1)}, u32[]{:S(2)}) copy-start(bf16[2,1024,1024]{2,1,0:T(8,128)(2,1)} %param.18) | copy-start | bytes 12582916
  745.4 98.0 %copy-start.28 = (f32[1024,1024]{1,0:T(8,128)S(1)}, f32[1024,1024]{1,0:T(8,128)}, u32[]{:S(2)}) copy-start(f32[1024,1024]{1,0:T(8,128)} %fusion.135) | copy-start | bytes 12582916
  745.4 98.0 %copy-start.29 = (f32[1024,1024]{1,0:T(8,128)S(1)}, f32[1024,1024]{1,0:T(8,128)}, u32[]{:S(2)}) copy-start(f32[1024,1024]{1,0:T(8,128)} %get-tuple-element.82) | copy-start | bytes 12582916
  745.4 98.0 %copy-start.171 = (f32[1024]{0:T(1024)S(1)}, f32[1024]{0:T(1024)}, u32[]{:S(2)}) copy-start(f32[1024]{0:T(1024)} %get-tuple-element.420) | copy-start | bytes 12292
  745.4 98.0 %copy-start.172 = (f32[1024]{0:T(1024)S(1)}, f32[1024]{0:T(1024)}, u32[]{:S(2)}) copy-start(f32[1024]{0:T(1024)} %get-tuple-element.466) | copy-start | bytes 12292
  863.6 21.3 %copy-start.1 = (bf16[1024,1024]{1,0:T(8,128)(2,1)S(1)}, bf16[1024,1024]{1,0:T(8,128)(2,1)}, u32[]{:S(2)}) copy-start(bf16[1024,1024]{1,0:T(8,128)(2,1)} %param.33) | copy-start | bytes 6291460
  (215 other events, 1103.3 us)
Sparse Core Ops, SparseCore 0:
  227.5 105.5 reduce-scatter.6
  588.5 133.1 all-reduce.99
  739.0 81.1 reduce-scatter.4
  863.7 19.6 all-reduce.97
